TPU v7x, 256 devices: a whole 4x4x8 slice. The times are simulated.
256 devices in a mesh: space: 32 (over x, z), grp: 8 (over y, core).
Axes of the slice: x: 4, y: 4, z: 8, core: 2. Of those that a mesh axis runs over, the one named last changes fastest.
Arguments:
- trial: bfloat16 [32768, 512], P(('space', 'grp')), may hold values from -11 to 11, as said below
- support: int32 [256, 2], P(('space', 'grp')), may hold values 0 or 1
- density: bfloat16 [32768, 1024], P(('space', 'grp')), may hold values from -0.25 to 0.25
- density_pattern: int32 [256, 8], P(('space', 'grp')), may hold values 0 or 1
- margin: bfloat16 [32768, 3072], P(('space', 'grp')), may hold values from -1 to 1, as said below
- margin_pattern: int32 [256, 24], P(('space', 'grp')), may hold values from 0 to 1, as said below
- pair_pattern: int32 [32, 3, 2, 2], P('space'), may hold values from 0 to 1, as said below
Outputs:
- orthonormal: float32 [32768, 1536], P(('space', 'grp'))
Inputs may be any that keep to these rules, and one draw needn't show every extreme that they name: trial is a float array; its rows of later domains tend to be larger. margin, read with margin_pattern, is a symmetric matrix over all 32768 orbitals with unit diagonal. `margin_pattern`: symmetric between atom blocks over all domains; every atom block is paired with itself. `pair_pattern`: symmetric between trial blocks over all domains; every trial block is paired with itself.
All inputs are finite; a program needn't handle non-finite values. No bound on the sum of `support` or of `density_pattern` on one device may be relied on, other than what follows from the above.
Results may differ from a plain program's by a relative error of at most 0.004.
Values may be sent and summed in bfloat16 or wider, within the bound.
No kernel may reach another device: no remote copies, remote signals or barrier semaphores. Data moves between devices by JAX's collectives and lax.ppermute only.
A program may use at most 64 MiB of HBM per device.

v0:
```python
import jax
import jax.numpy as jnp
from jax import lax
from jax.sharding import PartitionSpec as P


def padded(array, sides, width):
    for axis, dim in sides:
        devices, length = (lax.axis_size(axis), array.shape[dim])
        up = [(i, (i + 1) % devices) for i in range(devices)]
        down = [(j, i) for i, j in up]
        last = lax.slice_in_dim(array, length - width, length, axis=dim)
        leading = lax.slice_in_dim(array, 0, width, axis=dim)
        before = lax.ppermute(last, axis, up)
        after = lax.ppermute(leading, axis, down)
        array = jnp.concatenate([before, array, after], axis=dim)
    return array


def matmul_high(left_side, right_side):
    return jnp.dot(
        left_side, right_side, precision=lax.Precision.HIGHEST, preferred_element_type=jnp.float32
    )


def space_sides(band):
    return padded(band, (("space", 0),), 2)


def widen_whole(band):
    return space_sides(band)


def band_product(left_side, right_side, widen):
    widened = widen(right_side)
    lower = matmul_high(left_side[0], widened[0]) + matmul_high(left_side[1], widened[2])
    center = (
        matmul_high(left_side[0], widened[1])
        + matmul_high(left_side[1], widened[3])
        + matmul_high(left_side[2], widened[5])
    )
    upper = matmul_high(left_side[1], widened[4]) + matmul_high(left_side[2], widened[6])
    return jnp.stack([lower, center, upper])


def per_device(trial, support, density, density_pattern, margin, margin_pattern, pair_pattern):
    row_count = trial.shape[0]
    atom_count = support.shape[0]
    atom_orbs = row_count // atom_count
    trial_count = support.shape[1]
    trial_cols = trial.shape[1]
    trial_width = trial_cols // trial_count
    dom_rows = density.shape[1]
    dom_atoms = density_pattern.shape[1]
    support_mask = support.astype(jnp.bfloat16).reshape(atom_count, 1, trial_count, 1)
    trial_eff = (
        trial.reshape(atom_count, atom_orbs, trial_count, trial_width) * support_mask
    ).reshape(row_count, trial_cols)
    density_mask = density_pattern.astype(jnp.bfloat16).reshape(atom_count, 1, dom_atoms, 1)
    density_eff = (
        density.reshape(atom_count, atom_orbs, dom_atoms, atom_orbs) * density_mask
    ).reshape(row_count, dom_rows)
    projected = jnp.dot(
        density_eff,
        lax.all_gather(trial_eff, "grp", axis=0, tiled=True),
        preferred_element_type=jnp.float32,
    ).astype(jnp.bfloat16)
    margin_mask = margin_pattern.astype(jnp.bfloat16).reshape(atom_count, 1, 3, dom_atoms, 1)
    margin_eff = (
        margin.reshape(atom_count, atom_orbs, 3, dom_atoms, atom_orbs) * margin_mask
    ).reshape(row_count, 3, dom_rows)
    domain_psi = lax.all_gather(projected, "grp", axis=0, tiled=True)
    nearby = padded(domain_psi[None], (("space", 0),), 1)
    applied = jnp.einsum("rjc,jct->jrt", margin_eff, nearby, preferred_element_type=jnp.float32)
    applied = applied.astype(jnp.bfloat16)
    partial_sums = jnp.einsum("rt,jru->jtu", projected, applied, preferred_element_type=jnp.float32)
    pair_local = pair_pattern[0].astype(jnp.float32).reshape(3, trial_count, 1, trial_count, 1)
    pair_mask = jnp.broadcast_to(
        pair_local, (3, trial_count, trial_width, trial_count, trial_width)
    ).reshape(3, trial_cols, trial_cols)
    identity = jnp.eye(trial_cols, dtype=jnp.float32)
    nothing = jnp.zeros_like(identity)
    identity_band = jnp.stack([nothing, identity, nothing])
    blocks = lax.psum(partial_sums, "grp") * pair_mask
    peak = lax.pmax(jnp.max(jnp.diagonal(blocks[1])), "space")
    scaled = blocks / peak
    z_one = pair_mask * (1.5 * identity_band - 0.5 * scaled)
    square = pair_mask * band_product(z_one, z_one, widen_whole)
    weighed = pair_mask * band_product(scaled, square, widen_whole)
    z_two = pair_mask * (1.5 * z_one - 0.5 * band_product(z_one, weighed, widen_whole))
    result = jnp.einsum(
        "rt,jtu->rju", projected.astype(jnp.float32), z_two, precision=lax.Precision.HIGHEST
    )
    return result.reshape(row_count, 3 * trial_cols)


def solution(mesh):
    placed = (
        P(("space", "grp"), None),
        P(("space", "grp"), None),
        P(("space", "grp"), None),
        P(("space", "grp"), None),
        P(("space", "grp"), None),
        P(("space", "grp"), None),
        P("space", None, None, None),
    )
    return jax.shard_map(
        per_device, mesh=mesh, in_specs=placed, out_specs=P(("space", "grp"), None), check_vma=False
    )
```

profile of v0, /device:TPU:24, one launch (start us, length us, event | category | flops | bytes accessed | tf_op | source)
XLA Modules:
  0.0 423.7 jit_solution(4265930637378047454)
XLA Ops:
  9.7 26.5 %all-gather.3.cloned.1.call-done = bf16[1024,512]{1,0:T(8,128)(2,1)} async-done(((bf16[128,512]{1,0:T(8,128)(2,1)}), bf16[1024,512]{1,0:T(8,128)(2,1)}) %all-gather.3.cloned.1.call-update) | async-done | bytes 1048592 | tf_op jit(solution)/shard_map/all_gather | solution.py:65
  36.2 2.3 convolution_convert_fusion
  38.5 25.9 %all-gather.5.cloned.1.call-done = bf16[1024,512]{1,0:T(8,128)(2,1)} async-done(((bf16[128,512]{1,0:T(8,128)(2,1)}), bf16[1024,512]{1,0:T(8,128)(2,1)}) %all-gather.5.cloned.1.call-update) | async-done | bytes 1048592 | tf_op jit(solution)/shard_map/all_gather | solution.py:72
  64.4 5.4 %collective-permute-start.1 = (bf16[1,1024,512]{2,1,0:T(8,128)(2,1)}, bf16[1,1024,512]{2,1,0:T(8,128)(2,1)S(1)}, u32[]{:S(2)}, u32[]{:S(2)}) collective-permute-start(bf16[1,1024,512]{2,1,0:T(8,128)(2,1)} %bitcast.144), channel_id=1, source_target_pairs={{8,0},{16,8},{24,16},{32,24},{40,32},{48,40},{56,48},{64,56},{72,6... | collective-permute-start | bytes 3145736 | tf_op jit(solution)/shard_map/ppermute | solution.py:15
  72.2 20.8 %collective-permute-done.1 = bf16[1,1024,512]{2,1,0:T(8,128)(2,1)S(1)} collective-permute-done((bf16[1,1024,512]{2,1,0:T(8,128)(2,1)}, bf16[1,1024,512]{2,1,0:T(8,128)(2,1)S(1)}, u32[]{:S(2)}, u32[]{:S(2)}) %collective-permute-start.1) | collective-permute-done | bytes 1048608 | tf_op jit(solution)/shard_map/ppermute | solution.py:15
  93.0 5.4 %collective-permute-done = bf16[1,1024,512]{2,1,0:T(8,128)(2,1)S(1)} collective-permute-done((bf16[1,1024,512]{2,1,0:T(8,128)(2,1)}, bf16[1,1024,512]{2,1,0:T(8,128)(2,1)S(1)}, u32[]{:S(2)}, u32[]{:S(2)}) %collective-permute-start) | collective-permute-done | bytes 1048608 | tf_op jit(solution)/shard_map/ppermute | solution.py:14
  98.4 5.1 %convolution_bitcast_fusion = f32[3,512,512]{1,2,0:T(8,128)} fusion(bf16[1,1024,512]{2,1,0:T(8,128)(2,1)S(1)} %collective-permute-done.1, bf16[1,1024,512]{2,1,0:T(8,128)(2,1)} %bitcast.146, bf16[1,1024,512]{2,1,0:T(8,128)(2,1)S(1)} %collective-permute-done, bf16[128,3,1024]{0,2,1:T(8,128)(2,1)S(1)} %bitcast.141, bf16[3,1024]{1,0:T(4,128)(2,1)S(1)} %bitcast.142, ...), kind=kOutput, calls=%fused_computation.21 | convolution fusion | flops 607715328 | bytes 7215104 | tf_op jit(solution)/shard_map/rt,jru->jtu/dot_general | solution.py:76
  104.3 2.6 broadcast_in_dim.12
  106.9 4.2 reshape.60
  111.0 58.8 %all-reduce.2.cloned.1.call-done = f32[3,512,512]{1,2,0:T(8,128)} async-done(((f32[3,512,512]{1,2,0:T(8,128)}), f32[3,512,512]{1,2,0:T(8,128)}) %all-reduce.2.cloned.1.call-update) | async-done | bytes 3145744 | tf_op jit(solution)/shard_map/psum | solution.py:84
  169.8 2.6 mul.94
  175.1 8.7 %gather_fusion = f32[512]{0:T(512)S(1)} fusion(f32[512,512]{0,1:T(8,128)} %slice_bitcast_fusion.42, s32[512]{0:T(512)S(1)} %bitcast.139), kind=kCustom, calls=%fused_computation | custom fusion | bytes 8192 | tf_op jit(solution)/shard_map/jit(diagonal)/cond/branch_0_fun/gather | solution.py:85
  185.7 75.6 %pmax.7 = f32[]{:T(128)} all-reduce(f32[]{:T(128)} %reduce_max.9), channel_id=1, replica_groups=mesh['space'=32,'grp'=8] {'space'}, use_global_device_ids=true, to_apply=%region_2.3 | all-reduce | flops 1 | bytes 8 | tf_op jit(solution)/shard_map/pmax | solution.py:85
  261.4 4.1 fusion.1
  266.2 2.2 collective-permute-start.2
  274.1 27.2 %collective-permute-done.3 = f32[2,512,512]{1,2,0:T(8,128)S(1)} collective-permute-done((f32[2,512,512]{1,2,0:T(8,128)S(1)}, f32[2,512,512]{1,2,0:T(8,128)S(1)}, u32[]{:S(2)}, u32[]{:S(2)}) %collective-permute-start.3) | collective-permute-done | bytes 2097184 | tf_op jit(solution)/shard_map/ppermute | solution.py:15
  307.0 12.4 %fusion.29 = f32[1,512,512]{1,2,0:T(8,128)S(1)} fusion(f32[512,512]{0,1:T(8,128)S(1)} %fusion.44, f32[512,512]{0,1:T(8,128)S(1)} %fusion.50, f32[2,512,512]{1,2,0:T(8,128)S(1)} %collective-permute-done.2, f32[3,512,512]{1,2,0:T(8,128)S(1)} %get-tuple-element.5), kind=kOutput, calls=%fused_computation.43 | convolution fusion | flops 1611137024 | bytes 5242880 | tf_op jit(solution)/shard_map/dot_general | solution.py:21
  320.7 3.7 collective-permute-start.5
  330.0 26.4 %collective-permute-done.5 = f32[2,512,512]{1,2,0:T(8,128)S(1)} collective-permute-done((f32[2,512,512]{1,2,0:T(8,128)S(1)}, f32[2,512,512]{1,2,0:T(8,128)S(1)}, u32[]{:S(2)}, u32[]{:S(2)}) %collective-permute-start.5) | collective-permute-done | bytes 2097184 | tf_op jit(solution)/shard_map/ppermute | solution.py:15
  363.8 2.1 fusion.25
  367.2 4.1 collective-permute-start.7
  377.0 25.4 %collective-permute-done.7 = f32[2,512,512]{1,2,0:T(8,128)S(1)} collective-permute-done((f32[2,512,512]{1,2,0:T(8,128)S(1)}, f32[2,512,512]{1,2,0:T(8,128)S(1)}, u32[]{:S(2)}, u32[]{:S(2)}) %collective-permute-start.7) | collective-permute-done | bytes 2097184 | tf_op jit(solution)/shard_map/ppermute | solution.py:15
  411.8 2.8 fusion.10
  414.5 2.3 copy.56
  (61 shorter events, 53.3 us)
Async XLA Ops:
  6.5 29.6 %all-gather.3.cloned.1.call-start = ((), (), s32[]{:S(2)}) async-start(), calls=%async_computation | async-start | bytes 1179648 | tf_op jit(solution)/shard_map/all_gather | solution.py:65
  8.9 55.5 %all-gather.5.cloned.1.call-start = ((), (), s32[]{:S(2)}) async-start(), calls=%async_computation.1 | async-start | bytes 1179648 | tf_op jit(solution)/shard_map/all_gather | solution.py:72
  38.5 131.3 %all-reduce.2.cloned.1.call-start = ((), (), s32[]{:S(2)}) async-start(), calls=%async_computation.2 | async-start | bytes 6291456 | tf_op jit(solution)/shard_map/psum | solution.py:84
  64.4 28.6 %collective-permute-start.1 = (bf16[1,1024,512]{2,1,0:T(8,128)(2,1)}, bf16[1,1024,512]{2,1,0:T(8,128)(2,1)S(1)}, u32[]{:S(2)}, u32[]{:S(2)}) collective-permute-start(bf16[1,1024,512]{2,1,0:T(8,128)(2,1)} %bitcast.144), channel_id=1, source_target_pairs={{8,0},{16,8},{24,16},{32,24},{40,32},{48,40},{56,48},{64,56},{72,6... | collective-permute-start | bytes 3145736 | tf_op jit(solution)/shard_map/ppermute | solution.py:15
  69.9 28.5 %collective-permute-start = (bf16[1,1024,512]{2,1,0:T(8,128)(2,1)}, bf16[1,1024,512]{2,1,0:T(8,128)(2,1)S(1)}, u32[]{:S(2)}, u32[]{:S(2)}) collective-permute-start(bf16[1,1024,512]{2,1,0:T(8,128)(2,1)} %bitcast.145), channel_id=1, source_target_pairs={{0,8},{8,16},{16,24},{24,32},{32,40},{40,48},{48,56},{56,64},{64,7... | collective-permute-start | bytes 3145736 | tf_op jit(solution)/shard_map/ppermute | solution.py:14
  103.5 0.7 copy-start.2
  172.4 1.6 copy-start
  266.1 35.2 %collective-permute-start.3 = (f32[2,512,512]{1,2,0:T(8,128)S(1)}, f32[2,512,512]{1,2,0:T(8,128)S(1)}, u32[]{:S(2)}, u32[]{:S(2)}) collective-permute-start(f32[2,512,512]{1,2,0:T(8,128)S(1)} %get-tuple-element.12), channel_id=1, source_target_pairs={{8,0},{16,8},{24,16},{32,24},{40,32},{48,40},{56,48},{64,56},{72,6... | collective-permute-start | bytes 6291464 | tf_op jit(solution)/shard_map/ppermute | solution.py:15
  266.2 38.9 %collective-permute-start.2 = (f32[2,512,512]{1,2,0:T(8,128)S(1)}, f32[2,512,512]{1,2,0:T(8,128)S(1)}, u32[]{:S(2)}, u32[]{:S(2)}) collective-permute-start(f32[2,512,512]{1,2,0:T(8,128)S(1)} %get-tuple-element.11), channel_id=1, source_target_pairs={{0,8},{8,16},{16,24},{24,32},{32,40},{40,48},{48,56},{56,64},{64,7... | collective-permute-start | bytes 6291464 | tf_op jit(solution)/shard_map/ppermute | solution.py:14
  320.7 35.7 %collective-permute-start.5 = (f32[2,512,512]{1,2,0:T(8,128)S(1)}, f32[2,512,512]{1,2,0:T(8,128)S(1)}, u32[]{:S(2)}, u32[]{:S(2)}) collective-permute-start(f32[2,512,512]{1,2,0:T(8,128)S(1)} %get-tuple-element.10), channel_id=1, source_target_pairs={{8,0},{16,8},{24,16},{32,24},{40,32},{48,40},{56,48},{64,56},{72,6... | collective-permute-start | bytes 6291464 | tf_op jit(solution)/shard_map/ppermute | solution.py:15
  324.4 37.5 %collective-permute-start.4 = (f32[2,512,512]{1,2,0:T(8,128)S(1)}, f32[2,512,512]{1,2,0:T(8,128)S(1)}, u32[]{:S(2)}, u32[]{:S(2)}) collective-permute-start(f32[2,512,512]{1,2,0:T(8,128)S(1)} %get-tuple-element.9), channel_id=1, source_target_pairs={{0,8},{8,16},{16,24},{24,32},{32,40},{40,48},{48,56},{56,64},{64,7... | collective-permute-start | bytes 6291464 | tf_op jit(solution)/shard_map/ppermute | solution.py:14
  367.2 35.2 %collective-permute-start.7 = (f32[2,512,512]{1,2,0:T(8,128)S(1)}, f32[2,512,512]{1,2,0:T(8,128)S(1)}, u32[]{:S(2)}, u32[]{:S(2)}) collective-permute-start(f32[2,512,512]{1,2,0:T(8,128)S(1)} %get-tuple-element.8), channel_id=1, source_target_pairs={{8,0},{16,8},{24,16},{32,24},{40,32},{48,40},{56,48},{64,56},{72,6... | collective-permute-start | bytes 6291464 | tf_op jit(solution)/shard_map/ppermute | solution.py:15
  371.4 36.6 %collective-permute-start.6 = (f32[2,512,512]{1,2,0:T(8,128)S(1)}, f32[2,512,512]{1,2,0:T(8,128)S(1)}, u32[]{:S(2)}, u32[]{:S(2)}) collective-permute-start(f32[2,512,512]{1,2,0:T(8,128)S(1)} %get-tuple-element.7), channel_id=1, source_target_pairs={{0,8},{8,16},{16,24},{24,32},{32,40},{40,48},{48,56},{56,64},{64,7... | collective-permute-start | bytes 6291464 | tf_op jit(solution)/shard_map/ppermute | solution.py:14
  409.9 1.9 copy-start.1
Sparse Core Ops, SparseCore 0:
  9.2 26.8 all-gather.2
  38.6 25.7 all-gather.4
  103.6 66.1 all-reduce.1
where the time goes:
time: 432 us; the launch traced here: 424 us
  waiting for transfers between devices  220 us (51%)
  blocking collectives  75.6 us (17%)
  matrix products  60.2 us (14%)
  local copies, waits for them, and re-layouts  24.9 us (6%)
  starting transfers between devices  15.7 us (4%)
  between operations  13.8 us (3%)
  other arithmetic  13.6 us (3%)
    ppermute x4, waiting for transfers between devices, padded(): after = lax.ppermute(leading, axis, down)  99.8 us
    pmax x1, blocking collectives, per_device(): peak = lax.pmax(jnp.max(jnp.diagonal(blocks[1])), 'space')  75.6 us
    psum x1, waiting for transfers between devices, per_device(): blocks = lax.psum(partial_sums, 'grp') * pair_mask  58.8 us
    dot_general x21, matrix products, matmul_high(): jnp.dot(left_side, right_side, precision=lax.Precision.HIGHEST, preferred...  50 us
    all_gather x1, waiting for transfers between devices, per_device(): lax.all_gather(trial_eff, 'grp', axis=0, tiled=True)  26.5 us
    all_gather x1, waiting for transfers between devices, per_device(): domain_psi = lax.all_gather(projected, 'grp', axis=0, tiled=True)  25.9 us
    ppermute x4, starting transfers between devices, padded(): after = lax.ppermute(leading, axis, down)  13.3 us
    ppermute x4, waiting for transfers between devices, padded(): before = lax.ppermute(last, axis, up)  8.94 us
  transfers between devices with their start and end apart: 11, of which 10 were waited for; matrix products, arithmetic and copies ran while one was open for 9% of the time, Pallas kernels for 0%

commit v1 on v0

--- a/solution.py
+++ b/solution.py
@@ -81,7 +81,7 @@
     identity = jnp.eye(trial_cols, dtype=jnp.float32)
     nothing = jnp.zeros_like(identity)
     identity_band = jnp.stack([nothing, identity, nothing])
-    blocks = lax.psum(partial_sums, "grp") * pair_mask
+    blocks = jnp.sum(lax.all_gather(partial_sums, "grp"), axis=0) * pair_mask
     peak = lax.pmax(jnp.max(jnp.diagonal(blocks[1])), "space")
     scaled = blocks / peak
     z_one = pair_mask * (1.5 * identity_band - 0.5 * scaled)

time: 432 us -> 497 us (1.15)
  waiting for transfers between devices: 220 us -> 266 us
  other arithmetic: 13.6 us -> 27.4 us
    all_gather x0 -> x1, waiting for transfers between devices: none -> 113 us  [per_device(): blocks = jnp.sum(lax.all_gather(partial_sums, 'grp'), axis=0) * pair_mask]
    psum x1 -> x0, waiting for transfers between devices: 58.8 us -> none  [per_device(): blocks = lax.psum(partial_sums, 'grp') * pair_mask]
    ppermute x4, waiting for transfers between devices: 99.8 us -> 75.5 us  [padded(): after = lax.ppermute(leading, axis, down)]
    ppermute x4, waiting for transfers between devices: 8.94 us -> 24.9 us  [padded(): before = lax.ppermute(last, axis, up)]
    reduce_sum x0 -> x1, other arithmetic: none -> 11.8 us  [per_device(): blocks = jnp.sum(lax.all_gather(partial_sums, 'grp'), axis=0) * pair_mask]
  transfers between devices with their start and end apart: 11 -> 11, of which waited for: 10 -> 9; matrix products, arithmetic and copies ran while one was open for 9% -> 8% of each run, Pallas kernels for 0% -> 0%
where the time goes in v1:
time: 497 us; the launch traced here: 487 us
  waiting for transfers between devices  266 us (54%)
  blocking collectives  76.1 us (15%)
  matrix products  58.5 us (12%)
  local copies, waits for them, and re-layouts  29.5 us (6%)
  other arithmetic  27.4 us (6%)
  starting transfers between devices  15.7 us (3%)
  between operations  13.9 us (3%)
    all_gather x1, waiting for transfers between devices, per_device(): blocks = jnp.sum(lax.all_gather(partial_sums, 'grp'), axis=0) * pair_mask  113 us
    pmax x1, blocking collectives, per_device(): peak = lax.pmax(jnp.max(jnp.diagonal(blocks[1])), 'space')  76.1 us
    ppermute x4, waiting for transfers between devices, padded(): after = lax.ppermute(leading, axis, down)  75.5 us
    dot_general x21, matrix products, matmul_high(): jnp.dot(left_side, right_side, precision=lax.Precision.HIGHEST, preferred...  49.8 us
    all_gather x1, waiting for transfers between devices, per_device(): lax.all_gather(trial_eff, 'grp', axis=0, tiled=True)  26.5 us
    all_gather x1, waiting for transfers between devices, per_device(): domain_psi = lax.all_gather(projected, 'grp', axis=0, tiled=True)  25.9 us
    ppermute x4, waiting for transfers between devices, padded(): before = lax.ppermute(last, axis, up)  24.9 us
    ppermute x4, starting transfers between devices, padded(): after = lax.ppermute(leading, axis, down)  11.8 us
  transfers between devices with their start and end apart: 11, of which 9 were waited for; matrix products, arithmetic and copies ran while one was open for 8% of the time, Pallas kernels for 0%

profile of v1, /device:TPU:24, one launch (start us, length us, event | category | flops | bytes accessed | tf_op | source)
XLA Modules:
  0.0 487.2 jit_solution(7205769688532729726)
XLA Ops:
  9.7 26.5 %all-gather.5.cloned.1.call-done = bf16[1024,512]{1,0:T(8,128)(2,1)} async-done(((bf16[128,512]{1,0:T(8,128)(2,1)}), bf16[1024,512]{1,0:T(8,128)(2,1)}) %all-gather.5.cloned.1.call-update) | async-done | bytes 1048592 | tf_op jit(solution)/shard_map/all_gather | solution.py:65
  38.5 25.9 %all-gather.7.cloned.1.call-done = bf16[1024,512]{1,0:T(8,128)(2,1)} async-done(((bf16[128,512]{1,0:T(8,128)(2,1)}), bf16[1024,512]{1,0:T(8,128)(2,1)}) %all-gather.7.cloned.1.call-update) | async-done | bytes 1048592 | tf_op jit(solution)/shard_map/all_gather | solution.py:72
  66.0 3.9 collective-permute-start.1
  69.9 2.3 copy.27
  72.3 21.3 %collective-permute-done = bf16[1,1024,512]{2,1,0:T(8,128)(2,1)S(1)} collective-permute-done((bf16[1,1024,512]{2,1,0:T(8,128)(2,1)}, bf16[1,1024,512]{2,1,0:T(8,128)(2,1)S(1)}, u32[]{:S(2)}, u32[]{:S(2)}) %collective-permute-start) | collective-permute-done | bytes 1048608 | tf_op jit(solution)/shard_map/ppermute | solution.py:14
  95.0 3.7 convolution_bitcast_fusion
  98.7 2.4 copy.30
  101.9 2.6 broadcast_in_dim.12
  104.5 4.1 reshape.59
  108.7 113.3 %all-gather.9.cloned.1.call-done = f32[24,512,512]{2,1,0:T(8,128)} async-done(((f32[3,512,512]{2,1,0:T(8,128)}), f32[24,512,512]{2,1,0:T(8,128)}) %all-gather.9.cloned.1.call-update) | async-done | bytes 25165840 | tf_op jit(solution)/shard_map/all_gather | solution.py:84
  222.0 11.8 %reduce_sum.9 = f32[3,512,512]{2,1,0:T(8,128)} reduce(f32[8,3,512,512]{3,2,1,0:T(8,128)} %bitcast.141, f32[]{:T(128)} %constant.4.clone.1), dimensions={0}, to_apply=%region_0.0 | reduce | flops 5505024 | bytes 28311556 | tf_op jit(solution)/shard_map/reduce_sum | solution.py:84
  233.8 2.6 mul.94
  239.1 8.7 %gather_fusion = f32[512]{0:T(512)S(1)} fusion(f32[512,512]{1,0:T(8,128)} %slice_bitcast_fusion.42, s32[512]{0:T(512)S(1)} %bitcast.140), kind=kCustom, calls=%fused_computation | custom fusion | bytes 8192 | tf_op jit(solution)/shard_map/jit(diagonal)/cond/branch_0_fun/gather | solution.py:85
  249.6 76.1 %pmax.7 = f32[]{:T(128)} all-reduce(f32[]{:T(128)} %reduce_max.9), channel_id=1, replica_groups=mesh['space'=32,'grp'=8] {'space'}, use_global_device_ids=true, to_apply=%region_2.3 | all-reduce | flops 1 | bytes 8 | tf_op jit(solution)/shard_map/pmax | solution.py:85
  325.8 4.0 fusion.1
  338.3 25.9 %collective-permute-done.3 = f32[2,512,512]{2,1,0:T(8,128)S(1)} collective-permute-done((f32[2,512,512]{2,1,0:T(8,128)S(1)}, f32[2,512,512]{2,1,0:T(8,128)S(1)}, u32[]{:S(2)}, u32[]{:S(2)}) %collective-permute-start.3) | collective-permute-done | bytes 2097184 | tf_op jit(solution)/shard_map/ppermute | solution.py:15
  369.8 12.2 %fusion.21 = f32[1,512,512]{2,1,0:T(8,128)S(1)} fusion(f32[512,512]{1,0:T(8,128)S(1)} %fusion.36, f32[512,512]{1,0:T(8,128)S(1)} %fusion.42, f32[2,512,512]{2,1,0:T(8,128)S(1)} %collective-permute-done.2, f32[3,512,512]{2,1,0:T(8,128)S(1)} %get-tuple-element.5), kind=kOutput, calls=%fused_computation.36 | convolution fusion | flops 1611137024 | bytes 5242880 | tf_op jit(solution)/shard_map/dot_general | solution.py:21
  383.4 3.7 collective-permute-start.5
  392.7 25.3 %collective-permute-done.5 = f32[2,512,512]{2,1,0:T(8,128)S(1)} collective-permute-done((f32[2,512,512]{2,1,0:T(8,128)S(1)}, f32[2,512,512]{2,1,0:T(8,128)S(1)}, u32[]{:S(2)}, u32[]{:S(2)}) %collective-permute-start.5) | collective-permute-done | bytes 2097184 | tf_op jit(solution)/shard_map/ppermute | solution.py:15
  428.9 4.1 collective-permute-start.7
  438.5 24.2 %collective-permute-done.7 = f32[2,512,512]{2,1,0:T(8,128)S(1)} collective-permute-done((f32[2,512,512]{2,1,0:T(8,128)S(1)}, f32[2,512,512]{2,1,0:T(8,128)S(1)}, u32[]{:S(2)}, u32[]{:S(2)}) %collective-permute-start.7) | collective-permute-done | bytes 2097184 | tf_op jit(solution)/shard_map/ppermute | solution.py:15
  472.3 2.8 fusion.10
  475.1 2.4 copy.40
  477.6 2.7 fusion.53
  (70 shorter events, 60.5 us)
Async XLA Ops:
  6.5 65.6 %copy-start.5 = (s32[1,24]{1,0:T(1,128)S(1)}, s32[1,24]{1,0:T(1,128)}, u32[]{:S(2)}) copy-start(s32[1,24]{1,0:T(1,128)} %param.12) | copy-start | bytes 292
  6.5 29.6 %all-gather.5.cloned.1.call-start = ((), (), s32[]{:S(2)}) async-start(), calls=%async_computation | async-start | bytes 1179648 | tf_op jit(solution)/shard_map/all_gather | solution.py:65
  8.9 55.5 %all-gather.7.cloned.1.call-start = ((), (), s32[]{:S(2)}) async-start(), calls=%async_computation.1 | async-start | bytes 1179648 | tf_op jit(solution)/shard_map/all_gather | solution.py:72
  38.5 183.6 %all-gather.9.cloned.1.call-start = ((), (), s32[]{:S(2)}) async-start(), calls=%async_computation.2 | async-start | bytes 28311552 | tf_op jit(solution)/shard_map/all_gather | solution.py:84
  64.4 29.2 %collective-permute-start = (bf16[1,1024,512]{2,1,0:T(8,128)(2,1)}, bf16[1,1024,512]{2,1,0:T(8,128)(2,1)S(1)}, u32[]{:S(2)}, u32[]{:S(2)}) collective-permute-start(bf16[1,1024,512]{2,1,0:T(8,128)(2,1)} %bitcast.146), channel_id=1, source_target_pairs={{0,8},{8,16},{16,24},{24,32},{32,40},{40,48},{48,56},{56,64},{64,7... | collective-permute-start | bytes 3145736 | tf_op jit(solution)/shard_map/ppermute | solution.py:14
  66.0 27.7 %collective-permute-start.1 = (bf16[1,1024,512]{2,1,0:T(8,128)(2,1)}, bf16[1,1024,512]{2,1,0:T(8,128)(2,1)S(1)}, u32[]{:S(2)}, u32[]{:S(2)}) collective-permute-start(bf16[1,1024,512]{2,1,0:T(8,128)(2,1)} %bitcast.147), channel_id=1, source_target_pairs={{8,0},{16,8},{24,16},{32,24},{40,32},{48,40},{56,48},{64,56},{72,6... | collective-permute-start | bytes 3145736 | tf_op jit(solution)/shard_map/ppermute | solution.py:15
  93.6 1.0 copy-start.3
  93.6 1.3 copy-start.4
  101.1 0.7 copy-start.2
  236.4 1.6 copy-start
  330.4 33.8 %collective-permute-start.3 = (f32[2,512,512]{2,1,0:T(8,128)S(1)}, f32[2,512,512]{2,1,0:T(8,128)S(1)}, u32[]{:S(2)}, u32[]{:S(2)}) collective-permute-start(f32[2,512,512]{2,1,0:T(8,128)S(1)} %get-tuple-element.12), channel_id=1, source_target_pairs={{8,0},{16,8},{24,16},{32,24},{40,32},{48,40},{56,48},{64,56},{72,6... | collective-permute-start | bytes 6291464 | tf_op jit(solution)/shard_map/ppermute | solution.py:15
  330.5 37.4 %collective-permute-start.2 = (f32[2,512,512]{2,1,0:T(8,128)S(1)}, f32[2,512,512]{2,1,0:T(8,128)S(1)}, u32[]{:S(2)}, u32[]{:S(2)}) collective-permute-start(f32[2,512,512]{2,1,0:T(8,128)S(1)} %get-tuple-element.11), channel_id=1, source_target_pairs={{0,8},{8,16},{16,24},{24,32},{32,40},{40,48},{48,56},{56,64},{64,7... | collective-permute-start | bytes 6291464 | tf_op jit(solution)/shard_map/ppermute | solution.py:14
  383.4 34.6 %collective-permute-start.5 = (f32[2,512,512]{2,1,0:T(8,128)S(1)}, f32[2,512,512]{2,1,0:T(8,128)S(1)}, u32[]{:S(2)}, u32[]{:S(2)}) collective-permute-start(f32[2,512,512]{2,1,0:T(8,128)S(1)} %get-tuple-element.10), channel_id=1, source_target_pairs={{8,0},{16,8},{24,16},{32,24},{40,32},{48,40},{56,48},{64,56},{72,6... | collective-permute-start | bytes 6291464 | tf_op jit(solution)/shard_map/ppermute | solution.py:15
  387.1 36.4 %collective-permute-start.4 = (f32[2,512,512]{2,1,0:T(8,128)S(1)}, f32[2,512,512]{2,1,0:T(8,128)S(1)}, u32[]{:S(2)}, u32[]{:S(2)}) collective-permute-start(f32[2,512,512]{2,1,0:T(8,128)S(1)} %get-tuple-element.9), channel_id=1, source_target_pairs={{0,8},{8,16},{16,24},{24,32},{32,40},{40,48},{48,56},{56,64},{64,7... | collective-permute-start | bytes 6291464 | tf_op jit(solution)/shard_map/ppermute | solution.py:14
  428.9 33.9 %collective-permute-start.7 = (f32[2,512,512]{2,1,0:T(8,128)S(1)}, f32[2,512,512]{2,1,0:T(8,128)S(1)}, u32[]{:S(2)}, u32[]{:S(2)}) collective-permute-start(f32[2,512,512]{2,1,0:T(8,128)S(1)} %get-tuple-element.8), channel_id=1, source_target_pairs={{8,0},{16,8},{24,16},{32,24},{40,32},{48,40},{56,48},{64,56},{72,6... | collective-permute-start | bytes 6291464 | tf_op jit(solution)/shard_map/ppermute | solution.py:15
  432.9 35.3 %collective-permute-start.6 = (f32[2,512,512]{2,1,0:T(8,128)S(1)}, f32[2,512,512]{2,1,0:T(8,128)S(1)}, u32[]{:S(2)}, u32[]{:S(2)}) collective-permute-start(f32[2,512,512]{2,1,0:T(8,128)S(1)} %get-tuple-element.7), channel_id=1, source_target_pairs={{0,8},{8,16},{16,24},{24,32},{32,40},{40,48},{48,56},{56,64},{64,7... | collective-permute-start | bytes 6291464 | tf_op jit(solution)/shard_map/ppermute | solution.py:14
  475.1 2.4 copy-start.1
Sparse Core Ops, SparseCore 0:
  9.2 26.8 all-gather.4
  38.6 25.7 all-gather.6
  101.3 120.6 all-gather.8
